TPU v7x, 512 devices: a whole 4x4x16 slice. The times are simulated.
512 devices in a mesh: seq: 64 (over z, y), head: 4 (over x), dp: 2 (over core).
Axes of the slice: x: 4, y: 4, z: 16, core: 2. Of those that a mesh axis runs over, the one named last changes fastest.
Arguments:
- queries: bfloat16 [2, 8192, 4096], P('dp', 'seq', 'head'), may hold values from -0.23925781 to 0.23925781
- key_rows: bfloat16 [2, 8192, 4096], P('dp', 'seq', 'head'), may hold values from -0.23925781 to 0.23925781
- values: bfloat16 [2, 8192, 4096], P('dp', 'seq', 'head'), may hold values from -6 to 6
- out_grad: bfloat16 [2, 8192, 4096], P('dp', 'seq', 'head'), may hold values from -6 to 6
- decay_rate: float32 [32], P('head'), may hold values from 4e-05 to 0.025, as said below
- rotation: float32 [4, 4096], P(None, 'head')
- refusal: float32 [4096, 2], P('head')
- proj_weight: float32 [4, 4096], P(None, 'head'), may hold values from -0.09375 to 0.09375
- proj_bias: float32 [4], replicated, may hold values from -4 to 4
- positions: int32 [2, 16], P('dp'), may hold values from 0 to 8191, as said below
Outputs:
- attended: bfloat16 [2, 8192, 4096], P('dp', 'seq', 'head')
- grad_query: bfloat16 [2, 8192, 4096], P('dp', 'seq', 'head')
- grad_key: bfloat16 [2, 8192, 4096], P('dp', 'seq', 'head')
- grad_value: bfloat16 [2, 8192, 4096], P('dp', 'seq', 'head')
- grad_rotation: float32 [4, 4096], P(None, 'head')
- grad_weight: float32 [4, 4096], P(None, 'head')
- grad_bias: float32 [4], replicated
Inputs may be any that keep to these rules, and one draw needn't show every extreme that they name: 16 distinct positions in ascending order; among them always 0, 4096 and 8191. `decay_rate`: one rate per head, the same at every position.
All inputs are finite; a program needn't handle non-finite values.
Results may differ from a plain program's by a relative error of at most 0.0032.
Values sent between devices are 32-bit elements; how exact they have to be, the bound alone decides.
No kernel may reach another device: no remote copies, remote signals or barrier semaphores. Data moves between devices by JAX's collectives and lax.ppermute only.
A program may use at most 128 MiB of HBM per device.

v0:
```python
import jax
import jax.numpy as jnp
from jax import lax
from jax.sharding import PartitionSpec as P

highest = lax.Precision.HIGHEST


def carried_in(x, axis, combine, identity, reverse):
    peers, place = (lax.axis_size(axis), lax.axis_index(axis))
    everything = jax.tree.map(lambda part: lax.all_gather(part, axis), x)
    start = jax.tree.map(
        lambda part, zero: jnp.broadcast_to(jnp.asarray(zero, part.dtype), part.shape), x, identity
    )

    def lap(k, before):
        at = peers - 1 - k if reverse else k
        reached = at > place if reverse else at < place
        new = combine(before, jax.tree.map(lambda part: part[at], everything))
        return jax.tree.map(lambda a, b: jnp.where(reached, a, b), new, before)

    return lax.fori_loop(0, peers, lap, start)


def decay_table(log_decay, count):
    offsets = jnp.arange(count)
    between = offsets[:, None] - offsets[None, :]
    powers = jnp.exp(jnp.maximum(between, 0).astype(jnp.float32)[None] * log_decay[:, None, None])
    return jnp.where(between[None] >= 0, powers, 0.0)


def gram_inverse(gram):
    determinant = gram[0, 0] * gram[1, 1] - gram[0, 1] * gram[1, 0]
    adjugate = jnp.stack(
        [jnp.stack([gram[1, 1], -gram[0, 1]]), jnp.stack([-gram[1, 0], gram[0, 0]])]
    )
    return adjugate / determinant


def chain_combine(earlier, later):
    return (earlier[0] * later[0], later[0][:, None, None] * earlier[1] + later[1])


def shards(
    queries,
    key_rows,
    values,
    out_grad,
    decay_rate,
    rotation,
    refusal,
    proj_weight,
    proj_bias,
    positions,
):
    group = queries.shape[1]
    local_width = queries.shape[2]
    local_heads = decay_rate.shape[0]
    head_size = local_width // local_heads
    query_heads = queries[0].reshape(group, local_heads, head_size)
    key_heads = key_rows[0].reshape(group, local_heads, head_size)
    grad_heads = out_grad[0].reshape(group, local_heads, head_size)
    places = lax.axis_index("seq") * group + jnp.arange(group, dtype=jnp.int32)
    selector = places[:, None] == positions[0][None, :]
    select_low = selector.astype(jnp.bfloat16)
    select_full = selector.astype(jnp.float32)
    picked = jnp.dot(select_low.T, values[0], preferred_element_type=jnp.float32)
    gram_part = jnp.dot(refusal.T, refusal, precision=highest)
    coupling_part = jnp.dot(rotation, refusal, precision=highest)
    gram, coupling = lax.psum((gram_part, coupling_part), "head")
    inverse = gram_inverse(gram)
    rotated = rotation - jnp.dot(
        jnp.dot(coupling, inverse, precision=highest), refusal.T, precision=highest
    )
    code = (
        lax.psum(jnp.dot(picked, (proj_weight - rotated).T, precision=highest), "head") + proj_bias
    )
    shift_rows = jnp.dot(code, rotated, precision=highest)
    moved = (
        values[0].astype(jnp.float32) + jnp.dot(select_full, shift_rows, precision=highest)
    ).astype(jnp.bfloat16)
    moved_heads = moved.reshape(group, local_heads, head_size)
    log_decay = jnp.log1p(-decay_rate)
    table = decay_table(log_decay, group)
    offsets = jnp.arange(group).astype(jnp.float32)
    enter = jnp.exp((offsets + 1.0)[:, None] * log_decay[None, :])
    leave = jnp.exp((group - offsets)[:, None] * log_decay[None, :])
    start_weight = jnp.exp(offsets[:, None] * log_decay[None, :])
    end_weight = jnp.exp((group - 1.0 - offsets)[:, None] * log_decay[None, :])
    keep = jnp.exp(group * log_decay)
    query_full = query_heads.astype(jnp.float32)
    key_full = key_heads.astype(jnp.float32)
    moved_full = moved_heads.astype(jnp.float32)
    grad_full = grad_heads.astype(jnp.float32)
    local_state = jnp.einsum(
        "shd,she->hde", key_full * end_weight[:, :, None], moved_full, precision=highest
    )
    local_grad = jnp.einsum(
        "thd,the->hde", query_full * start_weight[:, :, None], grad_full, precision=highest
    )
    blank = (jnp.ones_like(keep), jnp.zeros_like(local_state))
    entering = carried_in((keep, local_state), "seq", chain_combine, blank, False)[1]
    leaving = carried_in((keep, local_grad), "seq", chain_combine, blank, True)[1]
    scores = jnp.einsum("thd,shd->hts", query_heads, key_heads, preferred_element_type=jnp.float32)
    mixing = (scores * table).astype(jnp.bfloat16)
    inner = jnp.einsum("hts,she->the", mixing, moved_heads, preferred_element_type=jnp.float32)
    outer = enter[:, :, None] * jnp.einsum("thd,hde->the", query_full, entering, precision=highest)
    attended = (inner + outer).astype(jnp.bfloat16).reshape(1, group, local_width)
    grad_scores = jnp.einsum(
        "the,she->hts", grad_heads, moved_heads, preferred_element_type=jnp.float32
    )
    grad_mixing = (grad_scores * table).astype(jnp.bfloat16)
    grad_query = jnp.einsum(
        "hts,shd->thd", grad_mixing, key_heads, preferred_element_type=jnp.float32
    )
    grad_query = grad_query + enter[:, :, None] * jnp.einsum(
        "the,hde->thd", grad_full, entering, precision=highest
    )
    grad_key = jnp.einsum(
        "hts,thd->shd", grad_mixing, query_heads, preferred_element_type=jnp.float32
    )
    grad_key = grad_key + leave[:, :, None] * jnp.einsum(
        "she,hde->shd", moved_full, leaving, precision=highest
    )
    grad_moved = jnp.einsum("hts,the->she", mixing, grad_heads, preferred_element_type=jnp.float32)
    grad_moved = grad_moved + leave[:, :, None] * jnp.einsum(
        "shd,hde->she", key_full, leaving, precision=highest
    )
    grad_moved = grad_moved.reshape(group, local_width)
    picked_grad = jnp.dot(select_full.T, grad_moved, precision=highest)
    code_grad = lax.psum(jnp.dot(picked_grad, rotated.T, precision=highest), "head")
    rotated_grad = jnp.dot(code.T, picked_grad, precision=highest) - jnp.dot(
        code_grad.T, picked, precision=highest
    )
    projected = lax.psum(jnp.dot(rotated_grad, refusal, precision=highest), "head")
    rotation_part = rotated_grad - jnp.dot(
        jnp.dot(projected, inverse, precision=highest), refusal.T, precision=highest
    )
    weight_part = jnp.dot(code_grad.T, picked, precision=highest)
    bias_part = jnp.sum(code_grad, axis=0)
    grad_weight, grad_bias, grad_rotation = lax.psum(
        (weight_part, bias_part, rotation_part), ("seq", "dp")
    )
    value_fix = jnp.dot(code_grad, proj_weight - rotated, precision=highest)
    grad_value = (
        (grad_moved + jnp.dot(select_full, value_fix, precision=highest))
        .astype(jnp.bfloat16)
        .reshape(1, group, local_width)
    )
    grad_query = grad_query.astype(jnp.bfloat16).reshape(1, group, local_width)
    grad_key = grad_key.astype(jnp.bfloat16).reshape(1, group, local_width)
    return (attended, grad_query, grad_key, grad_value, grad_rotation, grad_weight, grad_bias)


def solution(mesh):
    return jax.shard_map(
        shards,
        mesh=mesh,
        in_specs=(
            P("dp", "seq", "head"),
            P("dp", "seq", "head"),
            P("dp", "seq", "head"),
            P("dp", "seq", "head"),
            P("head"),
            P(None, "head"),
            P("head", None),
            P(None, "head"),
            P(),
            P("dp", None),
        ),
        out_specs=(
            P("dp", "seq", "head"),
            P("dp", "seq", "head"),
            P("dp", "seq", "head"),
            P("dp", "seq", "head"),
            P(None, "head"),
            P(None, "head"),
            P(),
        ),
        check_vma=False,
    )
```

profile of v0, /device:TPU:2, one launch (start us, length us, event | category | flops | bytes accessed | tf_op | source)
XLA Modules:
  0.0 1008.6 jit_solution(10857134564750874823)
XLA Ops:
  9.5 1.3 dynamic-slice
  12.3 1.5 fusion.20
  14.9 13.6 %all-reduce.3 = (f32[4,2]{0,1:T(2,128)S(1)}, f32[2,2]{1,0:T(2,128)S(1)}) all-reduce(f32[4,2]{0,1:T(2,128)S(1)} %fusion.63, f32[2,2]{1,0:T(2,128)S(1)} %fusion.64), channel_id=1, replica_groups=mesh['seq'=64,'head'=4,'dp'=2] {'head'}, use_global_device_ids=true, to_apply=%region_0.0 | all-reduce | flops 12 | bytes 96 | tf_op jit(solution)/shard_map/psum | solution.py:70
  31.7 146.4 %all-reduce = f32[512]{0:T(512)S(1)} all-reduce(f32[512]{0:T(512)S(1)} %get-tuple-element.328), channel_id=2, replica_groups=mesh['seq'=64,'head'=4,'dp'=2] {'seq'}, use_global_device_ids=true, to_apply=%add | all-reduce | flops 512 | bytes 4096
  180.8 1.4 maximum_bitcast_fusion
  183.9 1.2 fusion.30
  186.4 127.3 %all-gather.8.cloned.1.call-done = f32[512,128,128]{2,1,0:T(8,128)} async-done(((f32[8,128,128]{2,1,0:T(8,128)}), f32[512,128,128]{2,1,0:T(8,128)}) %all-gather.8.cloned.1.call-update) | async-done | bytes 33554448 | tf_op jit(solution)/shard_map/all_gather | solution.py:11
  313.7 78.5 %while.31 = (s32[]{:T(128)}, f32[8,128,128]{2,1,0:T(8,128)S(1)}, s32[]{:T(128)}, f32[64,8]{1,0:T(8,128)S(1)}, f32[64,8,128,128]{3,2,1,0:T(8,128)}, /*index=5*/s32[]{:T(128)}, s32[]{:T(128)}, s32[]{:T(128)}, s32[]{:T(128)}) while((s32[]{:T(128)}, f32[8,128,128]{2,1,0:T(8,128)S(1)}, s32[]{:T(128)}, f32[64,8]{1,0:T(8,128)S(1)}, ...), condition=%wide.region_6.7_spmd.clone, body=%wide.region_5.6_spmd.clone.sunk | while | flops 524296 | bytes 1573127 | solution.py:22
  318.6 1.2 fusion.114
  324.7 1.2 fusion.114
  333.3 1.2 fusion.114
  341.9 1.2 fusion.114
  348.1 1.2 fusion.114
  356.6 1.2 fusion.114
  365.2 1.2 fusion.114
  371.4 1.2 fusion.114
  394.3 8.6 all-reduce.2
  403.9 1.4 fusion.19
  405.3 1.2 fusion.23
  407.7 10.2 %psum.60 = f32[4,2]{0,1:T(2,128)S(1)} all-reduce(f32[4,2]{0,1:T(2,128)S(1)} %fusion.68), channel_id=1, replica_groups=mesh['seq'=64,'head'=4,'dp'=2] {'head'}, use_global_device_ids=true, to_apply=%region_8.9 | all-reduce | flops 8 | bytes 64 | tf_op jit(solution)/shard_map/psum | solution.py:135
  418.2 1.2 fusion.16
  422.3 495.7 %all-reduce.1 = (f32[4,1024]{1,0:T(4,128)}, f32[4,1024]{1,0:T(4,128)}, f32[4]{0:T(128)}) all-reduce(f32[4,1024]{1,0:T(4,128)S(1)} %convolution_subtract_fusion, f32[4,1024]{1,0:T(4,128)S(1)} %fusion.67, f32[4]{0:T(128)S(1)} %reduce_sum.9), channel_id=1, replica_groups=mesh['seq'=64,'head'=4,'dp'=2] {'seq','dp'}, use_global_device_ids=true, to_apply=%region_9.10 | all-reduce | flops 8196 | bytes 65568 | tf_op jit(solution)/shard_map/psum | solution.py:141
  919.0 1.8 fusion.18
  920.8 77.7 %while.30 = (s32[]{:T(128)}, f32[8,128,128]{2,1,0:T(8,128)S(1)}, s32[]{:T(128)}, f32[64,8]{1,0:T(8,128)S(1)}, f32[64,8,128,128]{3,2,1,0:T(8,128)}, /*index=5*/s32[]{:T(128)}, s32[]{:T(128)}) while((s32[]{:T(128)}, f32[8,128,128]{2,1,0:T(8,128)S(1)}, s32[]{:T(128)}, f32[64,8]{1,0:T(8,128)S(1)}, f32[64,8,128,128]{3,2,1,0:T(8,128)}, ...), condition=%wide.region_4.5_spmd.clone, body=%wide.region_3.4_spmd.clone.sunk | while | flops 524292 | bytes 1573065 | solution.py:22
  (313 shorter events, 162.9 us)
Async XLA Ops:
  7.2 6.7 copy-start
  7.2 306.5 %all-gather.8.cloned.1.call-start = ((), (), s32[]{:S(2)}) async-start(), calls=%async_computation.1 | async-start | bytes 34078720 | tf_op jit(solution)/shard_map/all_gather | solution.py:11
  12.2 301.5 %copy-start.5 = (f32[8]{0:T(128)}, f32[8]{0:T(128)S(1)}, u32[]{:S(2)}) copy-start(f32[8]{0:T(128)S(1)} %get-tuple-element.327) | copy-start | bytes 100
  13.8 907.0 %all-gather.6.cloned.1.call-start = ((), (), s32[]{:S(2)}) async-start(), calls=%async_computation | async-start | bytes 34078720 | tf_op jit(solution)/shard_map/all_gather | solution.py:11
  180.8 237.1 %copy-start.4 = (s32[128]{0:T(128)}, s32[128]{0:T(128)S(1)}, u32[]{:S(2)}) copy-start(s32[128]{0:T(128)S(1)} %iota_add_fusion) | copy-start | bytes 1540
  182.1 0.6 copy-start.6
  182.2 235.7 %copy-start.3 = (pred[128,128]{1,0:T(8,128)(4,1)}, pred[128,128]{1,0:T(8,128)(4,1)S(1)}, u32[]{:S(2)}) copy-start(pred[128,128]{1,0:T(8,128)(4,1)S(1)} %fusion.43) | copy-start | bytes 49156
  182.2 3.8 copy-start.1
  402.9 15.0 %copy-start.2 = (f32[16,4]{0,1:T(4,128)}, f32[16,4]{0,1:T(4,128)S(1)}, u32[]{:S(2)}) copy-start(f32[16,4]{0,1:T(4,128)S(1)} %get-tuple-element.316) | copy-start | bytes 772
Sparse Core Ops, SparseCore 0:
  13.9 299.7 all-gather.7
  406.6 291.8 all-gather.5
where the time goes:
time: 1020 us; the launch traced here: 1010 us
  blocking collectives  674 us (66%)
  other arithmetic  153 us (15%)
  waiting for transfers between devices  127 us (12%)
  matrix products  20.5 us (2%)
  between operations  18.9 us (2%)
    psum x1, blocking collectives, shards(): lax.psum((weight_part, bias_part, rotation_part), ('seq', 'dp'))  496 us
    select_n x128, other arithmetic, lap(): return jax.tree.map(lambda a, b: jnp.where(reached, a, b), new, before)  150 us
    unnamed x1, blocking collectives  146 us
    all_gather x2, waiting for transfers between devices, carried_in(): everything = jax.tree.map(lambda part: lax.all_gather(part, axis), x)  127 us
  transfers between devices with their start and end apart: 2, of which 1 were waited for; matrix products, arithmetic and copies ran while one was open for 2% of the time, Pallas kernels for 0%

commit v1 on v0

--- a/solution.py
+++ b/solution.py
@@ -139,7 +139,7 @@
     weight_part = jnp.dot(code_grad.T, picked, precision=highest)
     bias_part = jnp.sum(code_grad, axis=0)
     grad_weight, grad_bias, grad_rotation = lax.psum(
-        (weight_part, bias_part, rotation_part), ("seq", "dp")
+        lax.psum((weight_part, bias_part, rotation_part), "seq"), "dp"
     )
     value_fix = jnp.dot(code_grad, proj_weight - rotated, precision=highest)
     grad_value = (

time: 1020 us -> 804 us (0.79)
  the two profiles are of different devices: /device:TPU:2 before, /device:TPU:1 now
where the time goes in v1:
time: 804 us; the launch traced here: 797 us
  blocking collectives  435 us (54%)
  waiting for transfers between devices  155 us (19%)
  other arithmetic  153 us (19%)
  matrix products  20.6 us (3%)
  between operations  18.9 us (2%)
  local copies, waits for them, and re-layouts  9.93 us (1%)
    psum x1, blocking collectives, shards(): lax.psum((weight_part, bias_part, rotation_part), 'seq')  224 us
    all_gather x2, waiting for transfers between devices, carried_in(): everything = jax.tree.map(lambda part: lax.all_gather(part, axis), x)  155 us
    select_n x128, other arithmetic, lap(): return jax.tree.map(lambda a, b: jnp.where(reached, a, b), new, before)  150 us
    unnamed x1, blocking collectives  124 us
    psum x1, blocking collectives, shards(): lax.psum(lax.psum((weight_part, bias_part, rotation_part), 'seq'), 'dp')  64.2 us
  transfers between devices with their start and end apart: 2, of which 1 were waited for; matrix products, arithmetic and copies ran while one was open for 2% of the time, Pallas kernels for 0%

profile of v1, /device:TPU:1, one launch (start us, length us, event | category | flops | bytes accessed | tf_op | source)
XLA Modules:
  0.0 797.1 jit_solution(4369469670726650017)
XLA Ops:
  9.5 1.3 dynamic-slice
  12.3 1.5 fusion.20
  14.9 9.3 %all-reduce.3 = (f32[4,2]{0,1:T(2,128)S(1)}, f32[2,2]{1,0:T(2,128)S(1)}) all-reduce(f32[4,2]{0,1:T(2,128)S(1)} %fusion.63, f32[2,2]{1,0:T(2,128)S(1)} %fusion.64), channel_id=1, replica_groups=mesh['seq'=64,'head'=4,'dp'=2] {'head'}, use_global_device_ids=true, to_apply=%region_0.0 | all-reduce | flops 12 | bytes 96 | tf_op jit(solution)/shard_map/psum | solution.py:70
  27.4 123.5 %all-reduce = f32[512]{0:T(512)S(1)} all-reduce(f32[512]{0:T(512)S(1)} %get-tuple-element.331), channel_id=2, replica_groups=mesh['seq'=64,'head'=4,'dp'=2] {'seq'}, use_global_device_ids=true, to_apply=%add | all-reduce | flops 512 | bytes 4096
  153.6 1.4 maximum_bitcast_fusion
  156.7 1.2 fusion.30
  159.2 154.9 %all-gather.8.cloned.1.call-done = f32[512,128,128]{2,1,0:T(8,128)} async-done(((f32[8,128,128]{2,1,0:T(8,128)}), f32[512,128,128]{2,1,0:T(8,128)}) %all-gather.8.cloned.1.call-update) | async-done | bytes 33554448 | tf_op jit(solution)/shard_map/all_gather | solution.py:11
  314.1 78.5 %while.31 = (s32[]{:T(128)}, f32[8,128,128]{2,1,0:T(8,128)S(1)}, s32[]{:T(128)}, f32[64,8]{1,0:T(8,128)S(1)}, f32[64,8,128,128]{3,2,1,0:T(8,128)}, /*index=5*/s32[]{:T(128)}, s32[]{:T(128)}, s32[]{:T(128)}, s32[]{:T(128)}) while((s32[]{:T(128)}, f32[8,128,128]{2,1,0:T(8,128)S(1)}, s32[]{:T(128)}, f32[64,8]{1,0:T(8,128)S(1)}, ...), condition=%wide.region_6.7_spmd.clone, body=%wide.region_5.6_spmd.clone.sunk | while | flops 524296 | bytes 1573127 | solution.py:22
  316.5 1.2 fusion.114
  322.7 1.2 fusion.114
  331.3 1.2 fusion.114
  339.9 1.2 fusion.114
  346.0 1.2 fusion.114
  354.6 1.2 fusion.114
  363.2 1.2 fusion.114
  394.7 8.5 %all-reduce.2 = (f32[16,4]{0,1:T(4,128)S(1)}, f32[16,4]{0,1:T(4,128)S(1)}) all-reduce(f32[16,4]{0,1:T(4,128)S(1)} %fusion.55, f32[16,4]{0,1:T(4,128)S(1)} %fusion.66), channel_id=1, replica_groups=mesh['seq'=64,'head'=4,'dp'=2] {'head'}, use_global_device_ids=true, to_apply=%region_2.0 | all-reduce | flops 128 | bytes 1024 | tf_op jit(solution)/shard_map/psum | solution.py:76
  404.2 1.4 fusion.19
  405.6 1.2 fusion.23
  408.0 6.0 psum.81
  414.4 1.2 fusion.16
  418.4 223.7 %all-reduce.1 = (f32[4,1024]{1,0:T(4,128)S(1)}, f32[4,1024]{1,0:T(4,128)S(1)}, f32[4]{0:T(128)S(1)}) all-reduce(f32[4,1024]{1,0:T(4,128)S(1)} %convolution_subtract_fusion, f32[4,1024]{1,0:T(4,128)S(1)} %fusion.67, f32[4]{0:T(128)S(1)} %reduce_sum.9), channel_id=1, replica_groups=mesh['seq'=64,'head'=4,'dp'=2] {'seq'}, use_global_device_ids=true, to_apply=%region_9.10 | all-reduce | flops 8196 | bytes 65568 | tf_op jit(solution)/shard_map/psum | solution.py:142
  642.1 64.2 %all-reduce.4 = (f32[4,1024]{1,0:T(4,128)}, f32[4,1024]{1,0:T(4,128)}, f32[4]{0:T(128)}) all-reduce(f32[4,1024]{1,0:T(4,128)S(1)} %get-tuple-element.312, f32[4,1024]{1,0:T(4,128)S(1)} %get-tuple-element.313, f32[4]{0:T(128)S(1)} %get-tuple-element.314), channel_id=1, replica_groups=mesh['seq'=64,'head'=4,'dp'=2] {'dp'}, use_global_device_ids=true, to_apply=%region_10.11 | all-reduce | flops 8196 | bytes 65568 | tf_op jit(solution)/shard_map/psum | solution.py:141
  707.4 1.8 fusion.18
  709.2 77.7 %while.30 = (s32[]{:T(128)}, f32[8,128,128]{2,1,0:T(8,128)S(1)}, s32[]{:T(128)}, f32[64,8]{1,0:T(8,128)S(1)}, f32[64,8,128,128]{3,2,1,0:T(8,128)}, /*index=5*/s32[]{:T(128)}, s32[]{:T(128)}) while((s32[]{:T(128)}, f32[8,128,128]{2,1,0:T(8,128)S(1)}, s32[]{:T(128)}, f32[64,8]{1,0:T(8,128)S(1)}, f32[64,8,128,128]{3,2,1,0:T(8,128)}, ...), condition=%wide.region_4.5_spmd.clone, body=%wide.region_3.4_spmd.clone.sunk | while | flops 524292 | bytes 1573065 | solution.py:22
  (314 shorter events, 164.1 us)
Async XLA Ops:
  7.2 6.7 copy-start
  7.2 306.9 %all-gather.8.cloned.1.call-start = ((), (), s32[]{:S(2)}) async-start(), calls=%async_computation.1 | async-start | bytes 34078720 | tf_op jit(solution)/shard_map/all_gather | solution.py:11
  12.2 301.9 %copy-start.5 = (f32[8]{0:T(128)}, f32[8]{0:T(128)S(1)}, u32[]{:S(2)}) copy-start(f32[8]{0:T(128)S(1)} %get-tuple-element.330) | copy-start | bytes 100
  13.8 695.4 %all-gather.6.cloned.1.call-start = ((), (), s32[]{:S(2)}) async-start(), calls=%async_computation | async-start | bytes 34078720 | tf_op jit(solution)/shard_map/all_gather | solution.py:11
  153.6 260.5 %copy-start.4 = (s32[128]{0:T(128)}, s32[128]{0:T(128)S(1)}, u32[]{:S(2)}) copy-start(s32[128]{0:T(128)S(1)} %iota_add_fusion) | copy-start | bytes 1540
  155.0 0.6 copy-start.6
  155.0 259.0 %copy-start.3 = (pred[128,128]{1,0:T(8,128)(4,1)}, pred[128,128]{1,0:T(8,128)(4,1)S(1)}, u32[]{:S(2)}) copy-start(pred[128,128]{1,0:T(8,128)(4,1)S(1)} %fusion.43) | copy-start | bytes 49156
  155.0 3.8 copy-start.1
  403.2 10.9 %copy-start.2 = (f32[16,4]{0,1:T(4,128)}, f32[16,4]{0,1:T(4,128)S(1)}, u32[]{:S(2)}) copy-start(f32[16,4]{0,1:T(4,128)S(1)} %get-tuple-element.316) | copy-start | bytes 772
Sparse Core Ops, SparseCore 0:
  13.9 300.1 all-gather.7
  406.9 293.5 all-gather.5
